TPU v7x, 256 devices: a whole 4x4x8 slice. The times are simulated.
256 devices in a mesh: worker: 16 (over z, x_hi), fsdp: 8 (over y, core), tensor: 2 (over x_lo).
Axes of the slice: x: 4 (x_hi: 2, x_lo: 2; x = x_hi * 2 + x_lo), y: 4, z: 8, core: 2. Of those that a mesh axis runs over, the one named last changes fastest.
Arguments:
- tokens: bfloat16 [16, 1024, 2048], P('worker', 'fsdp', 'tensor'), may hold values from -6 to 6
- hidden_grad: bfloat16 [16, 1024, 7168], P('worker', None, ('fsdp', 'tensor')), may hold values from -6 to 6
- local_weights: bfloat16 [16, 2048, 2, 7168], P('worker', None, None, ('fsdp', 'tensor')), may hold values from -6 to 6
- anchor: float32 [2048, 2, 7168], P('worker', None, ('fsdp', 'tensor')), may hold values from -6 to 6
- momentum: float32 [2048, 2, 7168], P('worker', None, ('fsdp', 'tensor')), may hold values from -3 to 3
Outputs:
- updated: bfloat16 [16, 2048, 2, 7168], P('worker', None, None, ('fsdp', 'tensor'))
- anchor_out: float32 [2048, 2, 7168], P('worker', None, ('fsdp', 'tensor'))
- momentum_out: float32 [2048, 2, 7168], P('worker', None, ('fsdp', 'tensor'))
All inputs are finite; a program needn't handle non-finite values.
Results may differ from a plain program's by a relative error of at most 0.012.
Values may be sent and summed in bfloat16 or wider, within the bound.
A program may use at most 64 MiB of HBM per device.

v0:
```python
import math

import jax
import jax.numpy as jnp
from jax import lax
from jax.sharding import PartitionSpec as P

MIX_SHARE = 0.5
MOMENTUM_RATE = 0.9
OUTER_RATE = 0.7
INNER_RATE = 1.0


def pair_grad(gate_up, grad_rows):
    gate_part = gate_up[:, 0, :]
    up_part = gate_up[:, 1, :]
    sigmoid_gate = jax.nn.sigmoid(gate_part)
    upstream = grad_rows.astype(jnp.float32)
    grad_gate = upstream * up_part * sigmoid_gate * (1.0 + gate_part * (1.0 - sigmoid_gate))
    grad_up = upstream * gate_part * sigmoid_gate
    return jnp.stack([grad_gate, grad_up], axis=1).astype(jnp.bfloat16)


def body(tokens, hidden_grad, local_weights, anchor, momentum):
    workers = lax.axis_size("worker")
    weights_now = local_weights[0]
    row_count = weights_now.shape[0]
    weight_flat = weights_now.reshape(row_count, -1)
    features_all = lax.all_gather(tokens[0], "tensor", axis=1, tiled=True)
    gathered = lax.all_gather(features_all, "fsdp", axis=0, tiled=True)
    scaling = 1.0 / math.sqrt(row_count)
    own_part = jnp.dot(gathered, weight_flat, preferred_element_type=jnp.float32)
    summed = lax.psum_scatter(
        weights_now.astype(jnp.float32).astype(jnp.bfloat16),
        "worker",
        scatter_dimension=0,
        tiled=True,
    ).astype(jnp.float32)
    pseudo_grad = anchor - summed / workers
    momentum_out = MOMENTUM_RATE * momentum + pseudo_grad
    anchor_out = anchor - OUTER_RATE * (pseudo_grad + MOMENTUM_RATE * momentum_out)
    anchor_half = anchor_out.astype(jnp.bfloat16)
    anchor_full = lax.all_gather(anchor_half, "worker", axis=0, tiled=True).reshape(row_count, -1)
    outer_part = jnp.dot(gathered, anchor_full, preferred_element_type=jnp.float32)
    gate_up = (MIX_SHARE * own_part + (1.0 - MIX_SHARE) * outer_part) * scaling
    token_count = gate_up.shape[0]
    grad_pair = pair_grad(gate_up.reshape(token_count, 2, -1), hidden_grad[0]).reshape(
        token_count, -1
    )
    weight_grad = (
        lax.dot_general(
            gathered, grad_pair, (((0,), (0,)), ((), ())), preferred_element_type=jnp.float32
        )
        * scaling
    )
    merged = MIX_SHARE * weight_flat.astype(jnp.float32) + (1.0 - MIX_SHARE) * anchor_full.astype(
        jnp.float32
    )
    updated = (merged - INNER_RATE * weight_grad).astype(jnp.bfloat16).reshape(local_weights.shape)
    return (updated, anchor_out, momentum_out)


def solution(mesh):
    in_specs = (
        P("worker", "fsdp", "tensor"),
        P("worker", None, ("fsdp", "tensor")),
        P("worker", None, None, ("fsdp", "tensor")),
        P("worker", None, ("fsdp", "tensor")),
        P("worker", None, ("fsdp", "tensor")),
    )
    out_specs = (
        P("worker", None, None, ("fsdp", "tensor")),
        P("worker", None, ("fsdp", "tensor")),
        P("worker", None, ("fsdp", "tensor")),
    )
    return jax.shard_map(body, mesh=mesh, in_specs=in_specs, out_specs=out_specs, check_vma=False)
```

profile of v0, /device:TPU:8, one launch (start us, length us, event | category | flops | bytes accessed | tf_op | source)
XLA Modules:
  0.0 354.6 jit_solution(10893100304590473263)
XLA Ops:
  8.0 0.0 reduce-scatter.4.cloned.1.call-start
  8.0 6.1 %copy.10 = bf16[2048,896]{1,0:T(8,128)(2,1)} copy(bf16[2048,896]{0,1:T(8,128)(2,1)} %bitcast.36) | data formatting | bytes 7340032
  14.1 0.0 copy-start.4
  14.1 0.0 copy-start.2
  14.1 0.0 copy-start.3
  14.1 0.0 reduce-scatter.4.cloned.1.call-update
  14.1 0.0 all-gather.7.cloned.1.call-start
  14.2 0.9 copy-done.4
  15.1 8.8 %all-gather = bf16[1,128,2048]{2,1,0:T(8,128)(2,1)} all-gather(bf16[1,128,1024]{2,1,0:T(8,128)(2,1)S(1)} %copy-done.4), channel_id=2, replica_groups=mesh['worker'=16,'fsdp'=8,'tensor'=2] {'tensor'}, dimensions={2}, use_global_device_ids=true | all-gather | bytes 786432 | tf_op jit(solution)/shard_map/all_gather | solution.py:29
  23.9 0.0 all-gather.7.cloned.1.call-update
  23.9 0.0 all-gather.5.cloned.1.call-start
  23.9 205.3 %reduce-scatter.4.cloned.1.call-done = bf16[128,896]{1,0:T(8,128)(2,1)} async-done(((bf16[2048,896]{1,0:T(8,128)(2,1)}), bf16[128,896]{1,0:T(8,128)(2,1)}) %reduce-scatter.4.cloned.1.call-update) | async-done | bytes 229392
  229.2 1.1 copy.11
  230.4 0.0 copy-done.2
  230.4 0.0 copy-done.3
  230.4 1.1 fusion.17
  231.5 0.0 all-gather.5.cloned.1.call-update
  231.5 0.0 all-gather.7.cloned.1.call-done
  231.6 9.1 %fusion.5 = f32[1024,896]{0,1:T(8,128)} fusion(bf16[2048,896]{0,1:T(8,128)(2,1)} %bitcast.37, bf16[1,1024,2048]{2,1,0:T(8,128)(2,1)} %all-gather.7.cloned.1.call-done), kind=kOutput, calls=%fused_computation.6 | convolution fusion | flops 3758096384 | bytes 11534336 | tf_op jit(solution)/shard_map/dot_general | solution.py:32
  240.7 88.8 %all-gather.5.cloned.1.call-done = bf16[2048,2,448]{0,2,1:T(8,128)(2,1)} async-done(((bf16[128,2,448]{0,2,1:T(8,128)(2,1)}), bf16[2048,2,448]{0,2,1:T(8,128)(2,1)}) %all-gather.5.cloned.1.call-update) | async-done | bytes 3670032 | tf_op jit(solution)/shard_map/all_gather | solution.py:43
  329.5 0.0 copy-start.1
  329.5 0.0 copy-start.6
  329.5 8.5 %fusion.7 = f32[1024,896]{0,1:T(8,128)S(1)} fusion(f32[1024,896]{0,1:T(8,128)} %fusion.5, bf16[2048,896]{0,1:T(8,128)(2,1)} %bitcast.42, bf16[1,1024,2048]{2,1,0:T(8,128)(2,1)} %all-gather.7.cloned.1.call-done), kind=kOutput, calls=%fused_computation.9 | convolution fusion | flops 3759931392 | bytes 15204352 | tf_op jit(solution)/shard_map/dot_general | solution.py:44
  338.0 0.0 copy-done.1
  338.0 0.0 copy-start
  338.0 0.0 copy-start.5
  338.0 1.0 fusion.14
  339.0 0.2 pad_maximum_fusion
  339.2 0.0 copy-done.6
  339.2 0.9 copy-done
  340.1 1.3 copy-done.5
  341.3 5.8 %fusion = bf16[2048,896]{0,1:T(8,128)(2,1)} fusion(bf16[2048,896]{0,1:T(8,128)(2,1)S(1)} %bitcast.43, bf16[2048,896]{0,1:T(8,128)(2,1)S(1)} %bitcast.38, bf16[1024,896]{0,1:T(8,128)(2,1)S(1)} %bitcast.40, bf16[1,1024,2048]{2,1,0:T(8,128)(2,1)S(1)} %copy-done.5), kind=kOutput, calls=%fused_computation.1 | convolution fusion | flops 3770941440 | bytes 17039360 | tf_op jit(solution)/shard_map/dot_general | solution.py:51
Async XLA Ops:
  8.0 221.3 %reduce-scatter.4.cloned.1.call-start = ((), (), s32[]{:S(2)}) async-start(), calls=%async_computation.3 | async-start | bytes 3899392
  14.1 0.9 copy-start.4
  14.1 216.3 %copy-start.2 = (f32[128,2,448]{0,2,1:T(8,128)S(1)}, f32[128,2,448]{0,2,1:T(8,128)}, u32[]{:S(2)}) copy-start(f32[128,2,448]{0,2,1:T(8,128)} %param.8) | copy-start | bytes 1376260
  14.1 216.3 %copy-start.3 = (f32[128,2,448]{0,2,1:T(8,128)S(1)}, f32[128,2,448]{0,2,1:T(8,128)}, u32[]{:S(2)}) copy-start(f32[128,2,448]{0,2,1:T(8,128)} %param.9) | copy-start | bytes 1376260
  14.1 217.4 %all-gather.7.cloned.1.call-start = ((), (), s32[]{:S(2)}) async-start(), calls=%async_computation.2 | async-start | bytes 4718592 | tf_op jit(solution)/shard_map/all_gather | solution.py:30
  23.9 305.6 %all-gather.5.cloned.1.call-start = ((), (), s32[]{:S(2)}) async-start(), calls=%async_computation.1 | async-start | bytes 3899392 | tf_op jit(solution)/shard_map/all_gather | solution.py:43
  329.5 8.5 %copy-start.1 = (bf16[1,1024,448]{1,2,0:T(8,128)(2,1)S(1)}, bf16[1,1024,448]{1,2,0:T(8,128)(2,1)}, u32[]{:S(2)}) copy-start(bf16[1,1024,448]{1,2,0:T(8,128)(2,1)} %param.6) | copy-start | bytes 2752516
  329.5 9.7 %copy-start.6 = (bf16[2048,2,448]{0,2,1:T(8,128)(2,1)S(1)}, bf16[2048,2,448]{0,2,1:T(8,128)(2,1)}, u32[]{:S(2)}) copy-start(bf16[2048,2,448]{0,2,1:T(8,128)(2,1)} %all-gather.5.cloned.1.call-done) | copy-start | bytes 11010052
  338.0 2.0 copy-start
  338.0 3.3 copy-start.5
Sparse Core Ops, SparseCore 0:
  14.3 214.9 reduce-scatter.3
Sparse Core Ops, SparseCore 1:
  24.0 36.3 all-gather.6
  231.6 97.8 all-gather.4
where the time goes:
time: 355 us
  waiting for transfers between devices  294 us (83%)
  matrix products  23.5 us (7%)
  between operations  15.6 us (4%)
  local copies, waits for them, and re-layouts  10.2 us (3%)
  blocking collectives  8.82 us (2%)
    unnamed x4, waiting for transfers between devices  205 us
    all_gather x1, waiting for transfers between devices, body(): lax.all_gather(anchor_half, 'worker', axis=0, tiled=True)  88.8 us
    unnamed x16, local copies, waits for them, and re-layouts  10.2 us
    dot_general x1, matrix products, body(): jnp.dot(gathered, weight_flat, preferred_element_type=jnp.float32)  9.14 us
    all_gather x1, blocking collectives, body(): features_all = lax.all_gather(tokens[0], 'tensor', axis=1, tiled=True)  8.82 us
    dot_general x1, matrix products, body(): jnp.dot(gathered, anchor_full, preferred_element_type=jnp.float32)  8.48 us
  transfers between devices with their start and end apart: 3, of which 2 were waited for; matrix products, arithmetic and copies ran while one was open for 3% of the time, Pallas kernels for 0%

commit v1 on v0

v1 whole, which is shorter than its diff:
```python
import functools
import math

import jax
import jax.numpy as jnp
from jax import lax
from jax.experimental import pallas as pl
from jax.experimental.pallas import tpu as pltpu
from jax.sharding import PartitionSpec as P

MIX = 0.5
MOMENTUM_RATE = 0.9
OUTER_RATE = 0.7
D = 2048
FFL = 448
TOK = 1024
WORKERS = 16
SCALE = 1.0 / math.sqrt(D)
F32 = jnp.float32
BF16 = jnp.bfloat16
MESH = pl.DeviceIdType.MESH

CHUNKS = [
    (64, 1, 1, 3), (64, 0, 1, 4), (64, 1, 0, 3), (64, 0, 0, 4),
    (64, 1, 1, 3), (64, 0, 1, 4), (64, 1, 0, 3),
]
ORDER = [
    (-1, 0), (0, 0), (1, -1), (2, 0), (3, -1), (4, 0), (5, -1), (6, 0), (0, 1), (2, 1),
    (4, 1), (-1, 1), (6, 1), (0, 2), (2, 2), (4, 2), (-1, 2), (6, 2), (1, 0), (0, 3),
    (2, 3), (4, 3), (6, 3), (3, 0), (1, 1), (0, 4), (2, 4), (4, 4), (-1, 3), (5, 0),
    (6, 4), (-1, 5), (0, 5), (1, 2), (2, 5), (3, 1), (4, 5), (5, 1), (0, 7), (6, 5),
    (1, 3), (3, 2), (2, 6), (4, 7), (5, 2), (0, 8), (1, 5), (3, 3), (6, 6), (2, 7),
    (4, 8), (5, 3), (0, 9), (1, 7), (3, 5), (6, 7), (2, 8), (0, 10), (4, 9), (5, 5),
    (-1, 6), (1, 8), (3, 6), (6, 8), (-1, 4), (0, 11), (2, 9), (4, 10), (0, 12), (1, 9),
    (5, 7), (0, 13), (3, 7), (4, 11), (1, 10), (6, 9), (4, 12), (5, 8), (4, 13), (3, 8),
    (2, 11), (2, 12), (5, 9), (2, 13), (3, 9), (1, 11), (1, 12), (5, 10), (1, 13), (6, 11),
    (6, 12), (6, 13), (3, 11), (3, 12), (3, 13), (5, 11), (5, 12), (5, 13),
]


def kernel(tok, hgt, wt, ant, mot, upt, aot, mut,
           x_v, wz, an, mo, hg, rsr, rss, rsr1, rss1, xr, xs, xr8, az, own, mb, gp, ov,
           lsem, osem, gs, gr, rs_s, rs_r, ag_s, ag_r, xx_s, xx_r, ax_s, ax_r):
    w = lax.axis_index("worker")
    f = lax.axis_index("fsdp")
    t = lax.axis_index("tensor")
    z, xh, y, core = w // 2, w % 2, f // 2, f % 2
    xo = 1 - xh

    def dev(dz=0, dx=0, dy=0, dc=0, dt=0):
        return (((z + dz + 8) % 8) * 2 + (xh + dx) % 2,
                ((y + dy + 4) % 4) * 2 + (core + dc) % 2, (t + dt) % 2)

    zdev = (dev(dz=1), dev(dz=-1))
    xdev = dev(dx=1)
    ydevs = (dev(dy=1), dev(dy=-1), dev(dy=2))
    cdev = dev(dc=1)
    tdev = dev(dt=1)

    barrier = pltpu.get_barrier_semaphore()
    for d in (*zdev, xdev, *ydevs, cdev, tdev):
        pl.semaphore_signal(barrier, inc=1, device_id=d, device_id_type=MESH)

    loads = []

    def load(src, dst, k):
        c = pltpu.make_async_copy(src, dst, lsem.at[k])
        c.start()
        loads.append(c)

    def rowblock(ff):
        return pl.ds(pl.multiple_of(ff * 128, 128), 128)

    def colblock(tt):
        return pl.ds(pl.multiple_of(tt * 1024, 128), 1024)

    load(tok, x_v.at[rowblock(f), colblock(t)], 0)
    for zz in range(8):
        load(wt.at[:, :, pl.ds(zz * 256, 256)], wz.at[zz], 1 + zz)
    load(ant, an, 9)
    load(mot, mo, 10)
    load(hgt, hg, 11)
    for c in loads[:9]:
        c.wait()

    pl.semaphore_wait(barrier, 8)

    sent = []

    def copy(src, dst, ssem, rsem, to):
        return pltpu.make_async_remote_copy(src_ref=src, dst_ref=dst, send_sem=ssem, recv_sem=rsem,
                                            device_id=to, device_id_type=MESH)

    def send(src, dst, ssem, rsem, to):
        c = copy(src, dst, ssem, rsem, to)
        c.start()
        sent.append(c)

    def arrived(ref, rsem):
        copy(ref, ref, ssem=gs.at[0], rsem=rsem, to=cdev).wait_recv()

    def piece(ff, tt):
        return x_v.at[rowblock(ff), colblock(tt)]

    to = 1 - t
    fy = [((y + dy + 4) % 4) * 2 + core for dy in (-1, 1, -2)]

    def g_own():
        p = piece(f, t)
        send(p, p, gs.at[0], gr.at[0], tdev)
        for k in range(3):
            send(p, p, gs.at[1 + k], gr.at[1 + k], ydevs[k])
        send(p, p, gs.at[4], gr.at[4], cdev)

    def g_pair():
        p = piece(f, to)
        arrived(p, gr.at[0])
        for k in range(3):
            send(p, p, gs.at[5 + k], gr.at[5 + k], ydevs[k])
        send(p, p, gs.at[8], gr.at[8], cdev)

    def g_y(tt, k0, k1):
        for k in range(3):
            p = piece(fy[k], tt)
            arrived(p, gr.at[k0 + k])
            send(p, p, gs.at[k1 + k], gr.at[k1 + k], cdev)

    def g_end():
        fo = f + 1 - 2 * core
        arrived(piece(fo, t), gr.at[4])
        arrived(piece(fo, to), gr.at[8])
        for k in range(3):
            ff = fy[k] + 1 - 2 * core
            arrived(piece(ff, t), gr.at[9 + k])
            arrived(piece(ff, to), gr.at[12 + k])

    starts = [sum(r[0] for r in CHUNKS[:i]) for i in range(len(CHUNKS))]

    def lanes(h):
        return pl.ds(pl.multiple_of(h * 128, 128), 128)

    def zof(k):
        return (z + k + 16) % 8

    def run(c, name):
        R, rz, az_first, up = CHUNKS[c]
        rows = pl.ds(starts[c], R)
        dirs = ((0, 1, up), (1, -1, 7 - up))

        def f32(ref):
            return ref[...].astype(F32)

        if name == -1:
            send(wz.at[:, :, rows, lanes(xo)], xr8.at[:, :, rows], xx_s.at[c], xx_r.at[c], xdev)
        elif 0 <= name <= 3:
            s = name
            if not rz and s == 0:
                arrived(xr8.at[:, :, rows], xx_r.at[c])
            for d, sg, n in dirs:
                if s >= n:
                    continue
                zo = zof(sg * (n - s))
                k = d * 4 + s
                if rz:
                    src = wz.at[zo, :, rows]
                    if s > 0:
                        got = rsr.at[k - 1, :, rows]
                        arrived(got, rs_r.at[c, k - 1])
                        rss[k, :, rows] = (f32(src) + f32(got)).astype(BF16)
                        src = rss.at[k, :, rows]
                    send(src, rsr.at[k, :, rows], rs_s.at[c, k], rs_r.at[c, k], zdev[d])
                else:
                    total = f32(wz.at[zo, :, rows, lanes(xh)]) + f32(xr8.at[zo, :, rows])
                    if s > 0:
                        got = rsr1.at[k - 1, :, rows]
                        arrived(got, rs_r.at[c, k - 1])
                        total = total + f32(got)
                    rss1[k, :, rows] = total.astype(BF16)
                    send(rss1.at[k, :, rows], rsr1.at[k, :, rows], rs_s.at[c, k], rs_r.at[c, k], zdev[d])
        elif name == 4:
            for d, sg, n in dirs:
                arrived(rsr.at[d * 4 + n - 1, :, rows], rs_r.at[c, d * 4 + n - 1])

            def part(h):
                return (f32(wz.at[z, :, rows, lanes(h)]) + f32(rsr.at[up - 1, :, rows, lanes(h)])
                        + f32(rsr.at[4 + 6 - up, :, rows, lanes(h)]))

            xs[:, rows] = part(xo).astype(BF16)
            send(xs.at[:, rows], xr.at[:, rows], xx_s.at[c], xx_r.at[c], xdev)
            own[:, rows] = part(xh)
        elif name == 5:
            if rz:
                arrived(xr.at[:, rows], xx_r.at[c])
                total = own[:, rows] + f32(xr.at[:, rows])
            else:
                for d, sg, n in dirs:
                    arrived(rsr1.at[d * 4 + n - 1, :, rows], rs_r.at[c, d * 4 + n - 1])
                total = (f32(wz.at[z, :, rows, lanes(xh)]) + f32(xr8.at[z, :, rows])
                         + f32(rsr1.at[up - 1, :, rows]) + f32(rsr1.at[4 + 6 - up, :, rows]))
            anchor = an[:, rows]
            pseudo = anchor - total * (1.0 / WORKERS)
            mom = MOMENTUM_RATE * mo[:, rows] + pseudo
            new = anchor - OUTER_RATE * (pseudo + MOMENTUM_RATE * mom)
            mo[:, rows] = mom
            an[:, rows] = new
            az[z, xh, :, rows] = new.astype(BF16)
            mine = az.at[z, xh, :, rows]
            send(mine, mine, ax_s.at[c, 0], ax_r.at[c], xdev)
            if az_first:
                for d, sg, n in dirs:
                    send(mine, mine, ag_s.at[c, d * 4], ag_r.at[c, d * 4], zdev[d])
        elif 6 <= name <= 10:
            s = name - 6
            if not az_first and s == 0:
                arrived(az.at[z, xo, :, rows], ax_r.at[c])
            for d, sg, n in dirs:
                if s > n or (s == n and not az_first):
                    continue
                zo = zof(-sg * s)
                if az_first:
                    blk = az.at[zo, xh, :, rows]
                else:
                    blk = az.at[zo, :, :, rows]
                if s > 0:
                    arrived(blk, ag_r.at[c, d * 4 + s - 1])
                if s < n:
                    send(blk, blk, ag_s.at[c, d * 4 + s], ag_r.at[c, d * 4 + s], zdev[d])
                if az_first:
                    send(blk, blk, ax_s.at[c, d * up + s], ax_r.at[c], xdev)
        elif name == 11:
            if az_first:
                arrived(az.at[:, xo, :, rows], ax_r.at[c])
            else:
                for d, sg, n in dirs:
                    arrived(az.at[zof(-sg * n), :, :, rows], ag_r.at[c, d * 4 + n - 1])

            @pl.loop(0, 8)
            def _(zz):
                for h in range(2):
                    for p in range(2):
                        m = MIX * f32(wz.at[zz, p, rows, pl.ds(h * 128, 128)]) + (1.0 - MIX) * f32(az.at[zz, h, p, rows])
                        mb[pl.ds(p * R, R), pl.ds(pl.multiple_of(zz * 256 + h * 128, 128), 128)] = m.astype(BF16)
        elif name == 12:
            @pl.loop(0, 4)
            def _(i):
                tk = pl.ds(pl.multiple_of(i * 256, 256), 256)
                g = lax.dot_general(mb[pl.ds(0, 2 * R), :], x_v[tk, :], (((1,), (1,)), ((), ())),
                                    preferred_element_type=F32) * SCALE
                gate, upp = g[:R], g[R:]
                up_g = hg[rows, tk].astype(F32)
                sig = jax.nn.sigmoid(gate)
                gs_ = up_g * sig
                gp[pl.ds(0, R), tk] = (gs_ * upp * (1.0 + gate * (1.0 - sig))).astype(BF16)
                gp[pl.ds(R, R), tk] = (gs_ * gate).astype(BF16)
        elif name == 13:
            @pl.loop(0, 8)
            def _(zz):
                cols = pl.ds(pl.multiple_of(zz * 256, 256), 256)
                wg = jnp.dot(gp[pl.ds(0, 2 * R), :], x_v[:, cols], preferred_element_type=F32) * SCALE
                for p in range(2):
                    for h in range(2):
                        m = MIX * f32(wz.at[zz, p, rows, pl.ds(h * 128, 128)]) + (1.0 - MIX) * f32(az.at[zz, h, p, rows])
                        ov[p, rows, pl.ds(pl.multiple_of(zz * 256 + h * 128, 128), 128)] = (
                            m - wg[p * R:(p + 1) * R, h * 128:(h + 1) * 128]).astype(BF16)
            pltpu.make_async_copy(ov.at[:, rows], upt.at[:, rows], osem.at[c]).start()

    for c, name in ORDER:
        if c >= 0:
            run(c, name)
        elif name == 0:
            g_own()
        elif name == 1:
            g_pair()
        elif name == 2:
            g_y(t, 1, 9)
        elif name == 3:
            g_y(to, 5, 12)
        elif name == 4:
            g_end()
            loads[11].wait()
        elif name == 5:
            for l in loads[9:11]:
                l.wait()
        elif name == 6:
            pltpu.make_async_copy(an, aot, osem.at[len(CHUNKS)]).start()
            pltpu.make_async_copy(mo, mut, osem.at[len(CHUNKS) + 1]).start()

    for s in sent:
        s.wait_send()
    for c in range(len(CHUNKS)):
        rows = pl.ds(starts[c], CHUNKS[c][0])
        pltpu.make_async_copy(ov.at[:, rows], upt.at[:, rows], osem.at[c]).wait()
    pltpu.make_async_copy(an, aot, osem.at[len(CHUNKS)]).wait()
    pltpu.make_async_copy(mo, mut, osem.at[len(CHUNKS) + 1]).wait()


def body(tokens, hidden_grad, local_weights, anchor, momentum):
    n = len(CHUNKS)
    most = max(r[0] for r in CHUNKS)
    dma = pltpu.SemaphoreType.DMA
    hbm = pl.BlockSpec(memory_space=pl.ANY)
    up, an, mo = pl.pallas_call(
        kernel,
        name="outer_inner_step",
        out_shape=(
            jax.ShapeDtypeStruct((2, FFL, D), BF16),
            jax.ShapeDtypeStruct((2, FFL, 128), F32),
            jax.ShapeDtypeStruct((2, FFL, 128), F32),
        ),
        in_specs=[hbm] * 5,
        out_specs=(hbm,) * 3,
        scratch_shapes=[
            pltpu.VMEM((TOK, D), BF16),
            pltpu.VMEM((8, 2, FFL, 256), BF16),
            pltpu.VMEM((2, FFL, 128), F32),
            pltpu.VMEM((2, FFL, 128), F32),
            pltpu.VMEM((FFL, TOK), BF16),
            pltpu.VMEM((8, 2, FFL, 256), BF16),
            pltpu.VMEM((8, 2, FFL, 256), BF16),
            pltpu.VMEM((8, 2, FFL, 128), BF16),
            pltpu.VMEM((8, 2, FFL, 128), BF16),
            pltpu.VMEM((2, FFL, 128), BF16),
            pltpu.VMEM((2, FFL, 128), BF16),
            pltpu.VMEM((8, 2, FFL, 128), BF16),
            pltpu.VMEM((8, 2, 2, FFL, 128), BF16),
            pltpu.VMEM((2, FFL, 128), F32),
            pltpu.VMEM((2 * most, D), BF16),
            pltpu.VMEM((2 * most, TOK), BF16),
            pltpu.VMEM((2, FFL, D), BF16),
            dma((12,)),
            dma((n + 2,)),
            dma((15,)), dma((15,)),
            dma((n, 8)), dma((n, 8)),
            dma((n, 8)), dma((n, 8)),
            dma((n,)), dma((n,)),
            dma((n, 8)), dma((n,)),
        ],
        compiler_params=pltpu.CompilerParams(
            collective_id=0, has_side_effects=True, vmem_limit_bytes=56 << 20),
        cost_estimate=pl.CostEstimate(flops=4 * TOK * 2 * FFL * D, bytes_accessed=11_000_000, transcendentals=TOK * FFL),
    )(
        tokens[0],
        hidden_grad[0].T,
        local_weights[0].transpose(1, 2, 0),
        anchor.transpose(1, 2, 0),
        momentum.transpose(1, 2, 0),
    )
    return (up.transpose(2, 0, 1)[None], an.transpose(2, 0, 1), mo.transpose(2, 0, 1))


def solution(mesh):
    in_specs = (
        P("worker", "fsdp", "tensor"),
        P("worker", None, ("fsdp", "tensor")),
        P("worker", None, None, ("fsdp", "tensor")),
        P("worker", None, ("fsdp", "tensor")),
        P("worker", None, ("fsdp", "tensor")),
    )
    out_specs = (
        P("worker", None, None, ("fsdp", "tensor")),
        P("worker", None, ("fsdp", "tensor")),
        P("worker", None, ("fsdp", "tensor")),
    )
    return jax.shard_map(body, mesh=mesh, in_specs=in_specs, out_specs=out_specs, check_vma=False)
```

time: 355 us -> 98.3 us (0.28)
  waiting for transfers between devices: 294 us -> 0 us
  Pallas kernels: 0 us -> 91.5 us
  matrix products: 23.5 us -> 0 us
  between operations: 15.6 us -> 0.66 us
  blocking collectives: 8.82 us -> 0 us
  local copies, waits for them, and re-layouts: 10.2 us -> 5.99 us
    unnamed x4 -> x0, waiting for transfers between devices: 205 us -> none
    pallas_call x0 -> x1, Pallas kernels: none -> 91.5 us  [body(): pl.pallas_call(kernel, name='outer_inner_step', out_shape=(jax.ShapeDtype...]
    all_gather x2 -> x0, waiting for transfers between devices: 88.8 us -> none  [the longest x1 88.8 us: body(): lax.all_gather(anchor_half, 'worker', axis=0, tiled=True)]
    dot_general x3 -> x0, matrix products: 23.5 us -> none  [the longest x1 9.14 us: body(): jnp.dot(gathered, weight_flat, preferred_element_type=jnp.float32)]
    all_gather x1 -> x0, blocking collectives: 8.82 us -> none  [body(): features_all = lax.all_gather(tokens[0], 'tensor', axis=1, tiled=True)]
    unnamed x16 -> x7, local copies, waits for them, and re-layouts: 10.2 us -> 5.99 us
  transfers between devices with their start and end apart: 3 -> 0, of which waited for: 2 -> 0; matrix products, arithmetic and copies ran while one was open for 3% -> 0% of each run, Pallas kernels for 0% -> 0%
where the time goes in v1:
time: 98.3 us; the launch traced here: 98.2 us
  Pallas kernels  91.5 us (93%)
  local copies, waits for them, and re-layouts  5.99 us (6%)
    pallas_call x1, Pallas kernels, body(): pl.pallas_call(kernel, name='outer_inner_step', out_shape=(jax.ShapeDtype...  91.5 us
    unnamed x7, local copies, waits for them, and re-layouts  5.99 us

profile of v1, /device:TPU:8, one launch (start us, length us, event | category | flops | bytes accessed | tf_op | source)
XLA Modules:
  0.0 98.2 jit_solution(3941380727399967012)
XLA Ops:
  0.6 91.5 %outer_inner_step.1 = (bf16[2,448,2048]{2,1,0:T(8,128)(2,1)}, f32[2,448,128]{2,1,0:T(8,128)}, f32[2,448,128]{2,1,0:T(8,128)}) custom-call(bf16[128,1024]{1,0:T(8,128)(2,1)} %bitcast.21, bf16[448,1024]{1,0:T(8,128)(2,1)} %bitcast.18, bf16[2,448,2048]{2,1,0:T(8,128)(2,1)} %bitcast.17, f32[2,448,128]{2,1,0:T(8,128)} %bitcast.19, f32[2,448,128]{2,1,0:T(8,128)} %bitcast.20), custom_call_target="tpu_custom_call" | custom-call | flops 7516192768 | bytes 11000000 | tf_op jit(solution)/shard_map/outer_inner_step/pallas_call | solution.py:302
  92.2 0.0 copy-start.1
  92.2 0.0 copy-start
  92.2 4.5 %copy.11 = bf16[1,2048,2,448]{1,3,2,0:T(8,128)(2,1)} copy(bf16[1,2048,2,448]{1,3,2,0:T(8,128)(2,1)} %bitcast.14) | data formatting | bytes 7340032
  96.7 0.0 copy-done.1
  96.7 0.8 copy.12
  97.4 0.0 copy-done
  97.4 0.8 copy.13
Async XLA Ops:
  92.2 4.5 %copy-start.1 = (f32[2,448,128]{2,1,0:T(8,128)S(1)}, f32[2,448,128]{2,1,0:T(8,128)}, u32[]{:S(2)}) copy-start(f32[2,448,128]{2,1,0:T(8,128)} %get-tuple-element.7) | copy-start | bytes 1376260
  92.2 5.2 %copy-start = (f32[2,448,128]{2,1,0:T(8,128)S(1)}, f32[2,448,128]{2,1,0:T(8,128)}, u32[]{:S(2)}) copy-start(f32[2,448,128]{2,1,0:T(8,128)} %get-tuple-element.8) | copy-start | bytes 1376260

commit v2 on v1

--- a/solution.py
+++ b/solution.py
@@ -21,26 +21,27 @@
 MESH = pl.DeviceIdType.MESH
 
 CHUNKS = [
-    (64, 1, 1, 3), (64, 0, 1, 4), (64, 1, 0, 3), (64, 0, 0, 4),
-    (64, 1, 1, 3), (64, 0, 1, 4), (64, 1, 0, 3),
+    (48, 1, 1, 3), (48, 1, 1, 4), (80, 0, 1, 3), (80, 1, 1, 3),
+    (48, 0, 0, 4), (32, 1, 0, 4), (64, 1, 0, 4), (48, 0, 1, 4),
 ]
 ORDER = [
-    (-1, 0), (0, 0), (1, -1), (2, 0), (3, -1), (4, 0), (5, -1), (6, 0), (0, 1), (2, 1),
-    (4, 1), (-1, 1), (6, 1), (0, 2), (2, 2), (4, 2), (-1, 2), (6, 2), (1, 0), (0, 3),
-    (2, 3), (4, 3), (6, 3), (3, 0), (1, 1), (0, 4), (2, 4), (4, 4), (-1, 3), (5, 0),
-    (6, 4), (-1, 5), (0, 5), (1, 2), (2, 5), (3, 1), (4, 5), (5, 1), (0, 7), (6, 5),
-    (1, 3), (3, 2), (2, 6), (4, 7), (5, 2), (0, 8), (1, 5), (3, 3), (6, 6), (2, 7),
-    (4, 8), (5, 3), (0, 9), (1, 7), (3, 5), (6, 7), (2, 8), (0, 10), (4, 9), (5, 5),
-    (-1, 6), (1, 8), (3, 6), (6, 8), (-1, 4), (0, 11), (2, 9), (4, 10), (0, 12), (1, 9),
-    (5, 7), (0, 13), (3, 7), (4, 11), (1, 10), (6, 9), (4, 12), (5, 8), (4, 13), (3, 8),
-    (2, 11), (2, 12), (5, 9), (2, 13), (3, 9), (1, 11), (1, 12), (5, 10), (1, 13), (6, 11),
-    (6, 12), (6, 13), (3, 11), (3, 12), (3, 13), (5, 11), (5, 12), (5, 13),
+    (-1, 0), (0, 0), (1, 0), (2, -1), (3, 0), (0, 1), (1, 1), (4, -1), (5, 0), (3, 1),
+    (-1, 1), (0, 2), (1, 2), (5, 1), (3, 2), (0, 3), (1, 3), (5, 2), (-1, 2), (6, 0),
+    (3, 3), (2, 0), (0, 4), (1, 4), (5, 3), (7, -1), (6, 1), (4, 0), (5, 4), (-1, 5),
+    (0, 5), (1, 5), (2, 1), (3, 4), (6, 2), (4, 1), (0, 7), (1, 7), (2, 2), (-1, 3),
+    (7, 0), (5, 5), (6, 3), (4, 2), (0, 8), (3, 5), (1, 8), (2, 3), (7, 1), (5, 6),
+    (6, 4), (4, 3), (0, 9), (3, 7), (2, 5), (1, 9), (7, 2), (5, 7), (6, 5), (0, 10),
+    (4, 5), (3, 8), (2, 7), (1, 10), (7, 3), (5, 8), (3, 9), (6, 6), (2, 8), (-1, 4),
+    (0, 11), (7, 5), (5, 9), (4, 6), (0, 12), (3, 10), (0, 13), (6, 7), (2, 9), (1, 11),
+    (7, 7), (1, 12), (1, 13), (4, 7), (5, 11), (5, 12), (6, 8), (2, 10), (5, 13), (7, 8),
+    (3, 11), (4, 8), (3, 12), (6, 9), (3, 13), (7, 9), (2, 11), (4, 9), (2, 12), (2, 13),
+    (7, 10), (6, 11), (6, 12), (6, 13), (4, 11), (4, 12), (4, 13), (7, 11), (7, 12), (7, 13),
 ]
 
 
-def kernel(tok, hgt, wt, ant, mot, upt, aot, mut,
-           x_v, wz, an, mo, hg, rsr, rss, rsr1, rss1, xr, xs, xr8, az, own, mb, gp, ov,
-           lsem, osem, gs, gr, rs_s, rs_r, ag_s, ag_r, xx_s, xx_r, ax_s, ax_r):
+def kernel(tok, hgt, wt, ant, mot, ov, an, mo,
+           x_v, wz, hg, rsr, rss, rsr1, rss1, xr, xs, xr8, az, own, mb, gp,
+           lsem, gs, gr, rs_s, rs_r, ag_s, ag_r, xx_s, xx_r, ax_s, ax_r):
     w = lax.axis_index("worker")
     f = lax.axis_index("fsdp")
     t = lax.axis_index("tensor")
@@ -80,10 +81,14 @@
     load(ant, an, 9)
     load(mot, mo, 10)
     load(hgt, hg, 11)
-    for c in loads[:9]:
-        c.wait()
-
     pl.semaphore_wait(barrier, 8)
+    waited = []
+
+    def need(*ks):
+        for k in ks:
+            if k not in waited:
+                waited.append(k)
+                loads[k].wait()
 
     sent = []
 
@@ -107,10 +112,10 @@
 
     def g_own():
         p = piece(f, t)
-        send(p, p, gs.at[0], gr.at[0], tdev)
+        send(tok, p, gs.at[0], gr.at[0], tdev)
         for k in range(3):
-            send(p, p, gs.at[1 + k], gr.at[1 + k], ydevs[k])
-        send(p, p, gs.at[4], gr.at[4], cdev)
+            send(tok, p, gs.at[1 + k], gr.at[1 + k], ydevs[k])
+        send(tok, p, gs.at[4], gr.at[4], cdev)
 
     def g_pair():
         p = piece(f, to)
@@ -150,6 +155,10 @@
         def f32(ref):
             return ref[...].astype(F32)
 
+        if name == 0 and rz:
+            pass
+        else:
+            need(*range(1, 9))
         if name == -1:
             send(wz.at[:, :, rows, lanes(xo)], xr8.at[:, :, rows], xx_s.at[c], xx_r.at[c], xdev)
         elif 0 <= name <= 3:
@@ -163,7 +172,9 @@
                 k = d * 4 + s
                 if rz:
                     src = wz.at[zo, :, rows]
-                    if s > 0:
+                    if s == 0:
+                        src = wt.at[:, rows, pl.ds(pl.multiple_of(zo * 256, 256), 256)]
+                    else:
                         got = rsr.at[k - 1, :, rows]
                         arrived(got, rs_r.at[c, k - 1])
                         rss[k, :, rows] = (f32(src) + f32(got)).astype(BF16)
@@ -234,16 +245,14 @@
                 for d, sg, n in dirs:
                     arrived(az.at[zof(-sg * n), :, :, rows], ag_r.at[c, d * 4 + n - 1])
 
-            @pl.loop(0, 8)
-            def _(zz):
+            for zz in range(8):
                 for h in range(2):
                     for p in range(2):
                         m = MIX * f32(wz.at[zz, p, rows, pl.ds(h * 128, 128)]) + (1.0 - MIX) * f32(az.at[zz, h, p, rows])
-                        mb[pl.ds(p * R, R), pl.ds(pl.multiple_of(zz * 256 + h * 128, 128), 128)] = m.astype(BF16)
+                        mb[pl.ds(p * R, R), pl.ds(zz * 256 + h * 128, 128)] = m.astype(BF16)
         elif name == 12:
-            @pl.loop(0, 4)
-            def _(i):
-                tk = pl.ds(pl.multiple_of(i * 256, 256), 256)
+            for i in range(4):
+                tk = pl.ds(i * 256, 256)
                 g = lax.dot_general(mb[pl.ds(0, 2 * R), :], x_v[tk, :], (((1,), (1,)), ((), ())),
                                     preferred_element_type=F32) * SCALE
                 gate, upp = g[:R], g[R:]
@@ -253,16 +262,14 @@
                 gp[pl.ds(0, R), tk] = (gs_ * upp * (1.0 + gate * (1.0 - sig))).astype(BF16)
                 gp[pl.ds(R, R), tk] = (gs_ * gate).astype(BF16)
         elif name == 13:
-            @pl.loop(0, 8)
-            def _(zz):
-                cols = pl.ds(pl.multiple_of(zz * 256, 256), 256)
+            for zz in range(8):
+                cols = pl.ds(zz * 256, 256)
                 wg = jnp.dot(gp[pl.ds(0, 2 * R), :], x_v[:, cols], preferred_element_type=F32) * SCALE
                 for p in range(2):
                     for h in range(2):
                         m = MIX * f32(wz.at[zz, p, rows, pl.ds(h * 128, 128)]) + (1.0 - MIX) * f32(az.at[zz, h, p, rows])
-                        ov[p, rows, pl.ds(pl.multiple_of(zz * 256 + h * 128, 128), 128)] = (
+                        ov[p, rows, pl.ds(zz * 256 + h * 128, 128)] = (
                             m - wg[p * R:(p + 1) * R, h * 128:(h + 1) * 128]).astype(BF16)
-            pltpu.make_async_copy(ov.at[:, rows], upt.at[:, rows], osem.at[c]).start()
 
     for c, name in ORDER:
         if c >= 0:
@@ -277,21 +284,21 @@
             g_y(to, 5, 12)
         elif name == 4:
             g_end()
-            loads[11].wait()
+            need(0, 11)
         elif name == 5:
-            for l in loads[9:11]:
-                l.wait()
-        elif name == 6:
-            pltpu.make_async_copy(an, aot, osem.at[len(CHUNKS)]).start()
-            pltpu.make_async_copy(mo, mut, osem.at[len(CHUNKS) + 1]).start()
+            need(9, 10)
 
     for s in sent:
         s.wait_send()
-    for c in range(len(CHUNKS)):
-        rows = pl.ds(starts[c], CHUNKS[c][0])
-        pltpu.make_async_copy(ov.at[:, rows], upt.at[:, rows], osem.at[c]).wait()
-    pltpu.make_async_copy(an, aot, osem.at[len(CHUNKS)]).wait()
-    pltpu.make_async_copy(mo, mut, osem.at[len(CHUNKS) + 1]).wait()
+
+
+def store(ov, an, mo, upt, aot, mut, sem):
+    copies = [pltpu.make_async_copy(src, dst, sem.at[k])
+              for k, (src, dst) in enumerate(((ov, upt), (an, aot), (mo, mut)))]
+    for c in copies:
+        c.start()
+    for c in copies:
+        c.wait()
 
 
 def body(tokens, hidden_grad, local_weights, anchor, momentum):
@@ -303,17 +310,15 @@
         kernel,
         name="outer_inner_step",
         out_shape=(
-            jax.ShapeDtypeStruct((2, FFL, D), BF16),
-            jax.ShapeDtypeStruct((2, FFL, 128), F32),
-            jax.ShapeDtypeStruct((2, FFL, 128), F32),
+            pltpu.VMEM((2, FFL, D), BF16),
+            pltpu.VMEM((2, FFL, 128), F32),
+            pltpu.VMEM((2, FFL, 128), F32),
         ),
         in_specs=[hbm] * 5,
-        out_specs=(hbm,) * 3,
+        out_specs=(pl.BlockSpec(memory_space=pltpu.VMEM),) * 3,
         scratch_shapes=[
             pltpu.VMEM((TOK, D), BF16),
             pltpu.VMEM((8, 2, FFL, 256), BF16),
-            pltpu.VMEM((2, FFL, 128), F32),
-            pltpu.VMEM((2, FFL, 128), F32),
             pltpu.VMEM((FFL, TOK), BF16),
             pltpu.VMEM((8, 2, FFL, 256), BF16),
             pltpu.VMEM((8, 2, FFL, 256), BF16),
@@ -326,9 +331,7 @@
             pltpu.VMEM((2, FFL, 128), F32),
             pltpu.VMEM((2 * most, D), BF16),
             pltpu.VMEM((2 * most, TOK), BF16),
-            pltpu.VMEM((2, FFL, D), BF16),
             dma((12,)),
-            dma((n + 2,)),
             dma((15,)), dma((15,)),
             dma((n, 8)), dma((n, 8)),
             dma((n, 8)), dma((n, 8)),
@@ -336,7 +339,7 @@
             dma((n, 8)), dma((n,)),
         ],
         compiler_params=pltpu.CompilerParams(
-            collective_id=0, has_side_effects=True, vmem_limit_bytes=56 << 20),
+            collective_id=0, has_side_effects=True, vmem_limit_bytes=52 << 20),
         cost_estimate=pl.CostEstimate(flops=4 * TOK * 2 * FFL * D, bytes_accessed=11_000_000, transcendentals=TOK * FFL),
     )(
         tokens[0],
@@ -345,6 +348,19 @@
         anchor.transpose(1, 2, 0),
         momentum.transpose(1, 2, 0),
     )
+    up, an, mo = pl.pallas_call(
+        store,
+        name="store",
+        out_shape=(
+            jax.ShapeDtypeStruct((2, FFL, D), BF16),
+            jax.ShapeDtypeStruct((2, FFL, 128), F32),
+            jax.ShapeDtypeStruct((2, FFL, 128), F32),
+        ),
+        in_specs=[pl.BlockSpec(memory_space=pltpu.VMEM)] * 3,
+        out_specs=(hbm,) * 3,
+        scratch_shapes=[dma((3,))],
+        compiler_params=pltpu.CompilerParams(vmem_limit_bytes=8 << 20),
+    )(*(pltpu.with_memory_space_constraint(a, pltpu.VMEM) for a in (up, an, mo)))
     return (up.transpose(2, 0, 1)[None], an.transpose(2, 0, 1), mo.transpose(2, 0, 1))
 
 

time: 98.3 us -> 80.7 us (0.82)
  Pallas kernels: 91.5 us -> 79.7 us
  local copies, waits for them, and re-layouts: 5.99 us -> 0 us
    pallas_call x1 -> x2, Pallas kernels: 91.5 us -> 79.7 us  [the longest x1 77.5 us: body(): pl.pallas_call(kernel, name='outer_inner_step', out_shape=(pltpu.VMEM((2,...]
    unnamed x7 -> x0, local copies, waits for them, and re-layouts: 5.99 us -> none
where the time goes in v2:
time: 80.7 us; the launch traced here: 80.5 us
  Pallas kernels  79.7 us (99%)
    pallas_call x1, Pallas kernels, body(): pl.pallas_call(kernel, name='outer_inner_step', out_shape=(pltpu.VMEM((2,...  77.5 us
    pallas_call x1, Pallas kernels, body(): pl.pallas_call(store, name='store', out_shape=(jax.ShapeDtypeStruct((2, F...  2.15 us

profile of v2, /device:TPU:8, one launch (start us, length us, event | category | flops | bytes accessed | tf_op | source)
XLA Modules:
  0.0 80.5 jit_solution(14083283191624310709)
XLA Ops:
  0.6 77.5 %outer_inner_step.1 = (bf16[2,448,2048]{2,1,0:T(8,128)(2,1)S(1)}, f32[2,448,128]{2,1,0:T(8,128)S(1)}, f32[2,448,128]{2,1,0:T(8,128)S(1)}) custom-call(bf16[128,1024]{1,0:T(8,128)(2,1)} %bitcast.21, bf16[448,1024]{1,0:T(8,128)(2,1)} %bitcast.16, bf16[2,448,2048]{2,1,0:T(8,128)(2,1)} %bitcast.14, f32[2,448,128]{2,1,0:T(8,128)} %bitcast.17, f32[2,448,128]{2,1,0:T(8,128)} %bitcast.18), custom_call_target="tpu_custom_call" | custom-call | flops 7516192768 | bytes 11000000 | tf_op jit(solution)/shard_map/outer_inner_step/pallas_call | solution.py:309
  78.2 2.2 %store.1 = (bf16[2,448,2048]{2,1,0:T(8,128)(2,1)}, f32[2,448,128]{2,1,0:T(8,128)}, f32[2,448,128]{2,1,0:T(8,128)}) custom-call(bf16[2,448,2048]{2,1,0:T(8,128)(2,1)S(1)} %get-tuple-element.9.ov, f32[2,448,128]{2,1,0:T(8,128)S(1)} %get-tuple-element.10.an, f32[2,448,128]{2,1,0:T(8,128)S(1)} %get-tuple-element.11.mo), custom_call_target="tpu_custom_call" | custom-call | tf_op jit(solution)/shard_map/store/pallas_call | solution.py:351

commit v3 on v2

--- a/solution.py
+++ b/solution.py
@@ -29,18 +29,19 @@
     (-1, 1), (0, 2), (1, 2), (5, 1), (3, 2), (0, 3), (1, 3), (5, 2), (-1, 2), (6, 0),
     (3, 3), (2, 0), (0, 4), (1, 4), (5, 3), (7, -1), (6, 1), (4, 0), (5, 4), (-1, 5),
     (0, 5), (1, 5), (2, 1), (3, 4), (6, 2), (4, 1), (0, 7), (1, 7), (2, 2), (-1, 3),
-    (7, 0), (5, 5), (6, 3), (4, 2), (0, 8), (3, 5), (1, 8), (2, 3), (7, 1), (5, 6),
-    (6, 4), (4, 3), (0, 9), (3, 7), (2, 5), (1, 9), (7, 2), (5, 7), (6, 5), (0, 10),
-    (4, 5), (3, 8), (2, 7), (1, 10), (7, 3), (5, 8), (3, 9), (6, 6), (2, 8), (-1, 4),
-    (0, 11), (7, 5), (5, 9), (4, 6), (0, 12), (3, 10), (0, 13), (6, 7), (2, 9), (1, 11),
-    (7, 7), (1, 12), (1, 13), (4, 7), (5, 11), (5, 12), (6, 8), (2, 10), (5, 13), (7, 8),
-    (3, 11), (4, 8), (3, 12), (6, 9), (3, 13), (7, 9), (2, 11), (4, 9), (2, 12), (2, 13),
-    (7, 10), (6, 11), (6, 12), (6, 13), (4, 11), (4, 12), (4, 13), (7, 11), (7, 12), (7, 13),
+    (7, 0), (5, 5), (6, 3), (4, 2), (0, 8), (3, 5), (1, 8), (2, 3), (7, 1), (-1, 4),
+    (5, 6), (-1, 8), (6, 4), (4, 3), (0, 9), (-1, 9), (3, 7), (-1, 10), (2, 5), (1, 9),
+    (-1, 11), (7, 2), (5, 7), (6, 5), (0, 10), (4, 5), (3, 8), (2, 7), (1, 10), (7, 3),
+    (5, 8), (3, 9), (6, 6), (2, 8), (0, 11), (7, 5), (5, 9), (4, 6), (0, 12), (3, 10),
+    (0, 13), (6, 7), (2, 9), (1, 11), (7, 7), (1, 12), (1, 13), (4, 7), (5, 11), (5, 12),
+    (6, 8), (2, 10), (5, 13), (7, 8), (3, 11), (4, 8), (3, 12), (6, 9), (3, 13), (7, 9),
+    (2, 11), (4, 9), (2, 12), (2, 13), (7, 10), (6, 11), (6, 12), (6, 13), (4, 11), (4, 12),
+    (4, 13), (7, 11), (7, 12), (7, 13),
 ]
 
 
 def kernel(tok, hgt, wt, ant, mot, ov, an, mo,
-           x_v, wz, hg, rsr, rss, rsr1, rss1, xr, xs, xr8, az, own, mb, gp,
+           x_v, wz, hg, rsr, rss, rsr1, rss1, xr, xs, xr8, az, own, mb, gp, xt,
            lsem, gs, gr, rs_s, rs_r, ag_s, ag_r, xx_s, xx_r, ax_s, ax_r):
     w = lax.axis_index("worker")
     f = lax.axis_index("fsdp")
@@ -253,8 +254,7 @@
         elif name == 12:
             for i in range(4):
                 tk = pl.ds(i * 256, 256)
-                g = lax.dot_general(mb[pl.ds(0, 2 * R), :], x_v[tk, :], (((1,), (1,)), ((), ())),
-                                    preferred_element_type=F32) * SCALE
+                g = jnp.dot(mb[pl.ds(0, 2 * R), :], xt[:, tk], preferred_element_type=F32) * SCALE
                 gate, upp = g[:R], g[R:]
                 up_g = hg[rows, tk].astype(F32)
                 sig = jax.nn.sigmoid(gate)
@@ -287,6 +287,9 @@
             need(0, 11)
         elif name == 5:
             need(9, 10)
+        elif name >= 8:
+            for i in (2 * name - 16, 2 * name - 15):
+                xt[:, pl.ds(i * 128, 128)] = x_v[pl.ds(i * 128, 128), :].T
 
     for s in sent:
         s.wait_send()
@@ -331,6 +334,7 @@
             pltpu.VMEM((2, FFL, 128), F32),
             pltpu.VMEM((2 * most, D), BF16),
             pltpu.VMEM((2 * most, TOK), BF16),
+            pltpu.VMEM((D, TOK), BF16),
             dma((12,)),
             dma((15,)), dma((15,)),
             dma((n, 8)), dma((n, 8)),

time: 80.7 us -> 77.7 us (0.963)
  Pallas kernels: 79.7 us -> 76.9 us
    pallas_call x1, Pallas kernels: 77.5 us -> 74.7 us  [body(): pl.pallas_call(kernel, name='outer_inner_step', out_shape=(pltpu.VMEM((2,...]
where the time goes in v3:
time: 77.7 us
  Pallas kernels  76.9 us (99%)
  between operations  0.8 us (1%)
    pallas_call x1, Pallas kernels, body(): pl.pallas_call(kernel, name='outer_inner_step', out_shape=(pltpu.VMEM((2,...  74.7 us
    pallas_call x1, Pallas kernels, body(): pl.pallas_call(store, name='store', out_shape=(jax.ShapeDtypeStruct((2, F...  2.15 us

profile of v3, /device:TPU:8, one launch (start us, length us, event | category | flops | bytes accessed | tf_op | source)
XLA Modules:
  0.0 77.7 jit_solution(13579357076258148895)
XLA Ops:
  0.6 74.7 %outer_inner_step.1 = (bf16[2,448,2048]{2,1,0:T(8,128)(2,1)S(1)}, f32[2,448,128]{2,1,0:T(8,128)S(1)}, f32[2,448,128]{2,1,0:T(8,128)S(1)}) custom-call(bf16[128,1024]{1,0:T(8,128)(2,1)} %bitcast.21, bf16[448,1024]{1,0:T(8,128)(2,1)} %bitcast.16, bf16[2,448,2048]{2,1,0:T(8,128)(2,1)} %bitcast.14, f32[2,448,128]{2,1,0:T(8,128)} %bitcast.17, f32[2,448,128]{2,1,0:T(8,128)} %bitcast.18), custom_call_target="tpu_custom_call" | custom-call | flops 7516192768 | bytes 11000000 | tf_op jit(solution)/shard_map/outer_inner_step/pallas_call | solution.py:312
  75.3 2.2 %store.1 = (bf16[2,448,2048]{2,1,0:T(8,128)(2,1)}, f32[2,448,128]{2,1,0:T(8,128)}, f32[2,448,128]{2,1,0:T(8,128)}) custom-call(bf16[2,448,2048]{2,1,0:T(8,128)(2,1)S(1)} %get-tuple-element.9.ov, f32[2,448,128]{2,1,0:T(8,128)S(1)} %get-tuple-element.10.an, f32[2,448,128]{2,1,0:T(8,128)S(1)} %get-tuple-element.11.mo), custom_call_target="tpu_custom_call" | custom-call | tf_op jit(solution)/shard_map/store/pallas_call | solution.py:355

commit v4 on v3

--- a/solution.py
+++ b/solution.py
@@ -21,27 +21,37 @@
 MESH = pl.DeviceIdType.MESH
 
 CHUNKS = [
-    (48, 1, 1, 3), (48, 1, 1, 4), (80, 0, 1, 3), (80, 1, 1, 3),
-    (48, 0, 0, 4), (32, 1, 0, 4), (64, 1, 0, 4), (48, 0, 1, 4),
+    (32, 1, 1, 3), (96, 0, 0, 3), (80, 0, 1, 4), (48, 1, 1, 4),
+    (48, 1, 1, 4), (64, 1, 1, 3), (80, 1, 0, 4),
 ]
 ORDER = [
-    (-1, 0), (0, 0), (1, 0), (2, -1), (3, 0), (0, 1), (1, 1), (4, -1), (5, 0), (3, 1),
-    (-1, 1), (0, 2), (1, 2), (5, 1), (3, 2), (0, 3), (1, 3), (5, 2), (-1, 2), (6, 0),
-    (3, 3), (2, 0), (0, 4), (1, 4), (5, 3), (7, -1), (6, 1), (4, 0), (5, 4), (-1, 5),
-    (0, 5), (1, 5), (2, 1), (3, 4), (6, 2), (4, 1), (0, 7), (1, 7), (2, 2), (-1, 3),
-    (7, 0), (5, 5), (6, 3), (4, 2), (0, 8), (3, 5), (1, 8), (2, 3), (7, 1), (-1, 4),
-    (5, 6), (-1, 8), (6, 4), (4, 3), (0, 9), (-1, 9), (3, 7), (-1, 10), (2, 5), (1, 9),
-    (-1, 11), (7, 2), (5, 7), (6, 5), (0, 10), (4, 5), (3, 8), (2, 7), (1, 10), (7, 3),
-    (5, 8), (3, 9), (6, 6), (2, 8), (0, 11), (7, 5), (5, 9), (4, 6), (0, 12), (3, 10),
-    (0, 13), (6, 7), (2, 9), (1, 11), (7, 7), (1, 12), (1, 13), (4, 7), (5, 11), (5, 12),
-    (6, 8), (2, 10), (5, 13), (7, 8), (3, 11), (4, 8), (3, 12), (6, 9), (3, 13), (7, 9),
-    (2, 11), (4, 9), (2, 12), (2, 13), (7, 10), (6, 11), (6, 12), (6, 13), (4, 11), (4, 12),
-    (4, 13), (7, 11), (7, 12), (7, 13),
+    (-1, 0), (0, 0), (1, -1), (2, -1), (3, 0), (4, 0), (5, 0), (6, 0), (0, 1), (3, 1),
+    (4, 1), (-1, 1), (5, 1), (6, 1), (0, 2), (3, 2), (4, 2), (5, 2), (-1, 2), (1, 0),
+    (6, 2), (0, 3), (3, 3), (4, 3), (5, 3), (1, 1), (6, 3), (2, 0), (0, 4), (3, 4),
+    (4, 4), (5, 4), (-1, 3), (1, 2), (-1, 5), (0, 5), (6, 4), (3, 5), (2, 1), (4, 5),
+    (5, 5), (-1, 4), (1, 3), (-1, 8), (0, 7), (3, 7), (-1, 9), (6, 5), (2, 2), (-1, 10),
+    (4, 7), (5, 7), (-1, 11), (1, 5), (0, 8), (3, 8), (2, 3), (6, 6), (4, 8), (5, 8),
+    (0, 9), (3, 9), (2, 5), (1, 6), (6, 7), (4, 9), (0, 10), (5, 9), (3, 10), (2, 7),
+    (1, 7), (6, 8), (5, 10), (0, 11), (4, 10), (0, 12), (2, 8), (0, 13), (3, 11), (1, 8),
+    (3, 12), (3, 13), (6, 9), (5, 11), (5, 12), (2, 9), (5, 13), (1, 9), (4, 11), (4, 12),
+    (4, 13), (6, 11), (6, 12), (2, 10), (6, 13), (1, 11), (1, 12), (1, 13), (2, 11), (2, 12),
+    (2, 13),
 ]
 
-
-def kernel(tok, hgt, wt, ant, mot, ov, an, mo,
-           x_v, wz, hg, rsr, rss, rsr1, rss1, xr, xs, xr8, az, own, mb, gp, xt,
+LAST = [c for c, step in ORDER if c >= 0 and step == 11][-1]
+FIRST_ROW = sum(r[0] for r in CHUNKS[:LAST])
+LAST_ROWS = CHUNKS[LAST][0]
+
+
+def pair_grad(g, up_g, R):
+    gate, upp = g[:R], g[R:]
+    sig = jax.nn.sigmoid(gate)
+    scaled = up_g * sig
+    return (scaled * upp * (1.0 + gate * (1.0 - sig))).astype(BF16), (scaled * gate).astype(BF16)
+
+
+def kernel(tok, hgt, wt, ant, mot, ov, an, mo, x_v, xt, mbl, mfl, hg,
+           wz, rsr, rss, rsr1, rss1, xr, xs, xr8, az, own, mb, gp,
            lsem, gs, gr, rs_s, rs_r, ag_s, ag_r, xx_s, xx_r, ax_s, ax_r):
     w = lax.axis_index("worker")
     f = lax.axis_index("fsdp")
@@ -250,17 +260,17 @@
                 for h in range(2):
                     for p in range(2):
                         m = MIX * f32(wz.at[zz, p, rows, pl.ds(h * 128, 128)]) + (1.0 - MIX) * f32(az.at[zz, h, p, rows])
-                        mb[pl.ds(p * R, R), pl.ds(zz * 256 + h * 128, 128)] = m.astype(BF16)
+                        to_row, to_col = pl.ds(p * R, R), pl.ds(zz * 256 + h * 128, 128)
+                        if c == LAST:
+                            mbl[to_row, to_col] = m.astype(BF16)
+                            mfl[to_row, to_col] = m
+                        else:
+                            mb[to_row, to_col] = m.astype(BF16)
         elif name == 12:
             for i in range(4):
                 tk = pl.ds(i * 256, 256)
                 g = jnp.dot(mb[pl.ds(0, 2 * R), :], xt[:, tk], preferred_element_type=F32) * SCALE
-                gate, upp = g[:R], g[R:]
-                up_g = hg[rows, tk].astype(F32)
-                sig = jax.nn.sigmoid(gate)
-                gs_ = up_g * sig
-                gp[pl.ds(0, R), tk] = (gs_ * upp * (1.0 + gate * (1.0 - sig))).astype(BF16)
-                gp[pl.ds(R, R), tk] = (gs_ * gate).astype(BF16)
+                gp[pl.ds(0, R), tk], gp[pl.ds(R, R), tk] = pair_grad(g, hg[rows, tk].astype(F32), R)
         elif name == 13:
             for zz in range(8):
                 cols = pl.ds(zz * 256, 256)
@@ -272,8 +282,12 @@
                             m - wg[p * R:(p + 1) * R, h * 128:(h + 1) * 128]).astype(BF16)
 
     for c, name in ORDER:
+        if c == LAST and name > 11:
+            continue
         if c >= 0:
             run(c, name)
+            for _ in range(min(4, max(0, len(sent) - 40))):
+                sent.pop(0).wait_send()
         elif name == 0:
             g_own()
         elif name == 1:
@@ -295,12 +309,29 @@
         s.wait_send()
 
 
-def store(ov, an, mo, upt, aot, mut, sem):
-    copies = [pltpu.make_async_copy(src, dst, sem.at[k])
-              for k, (src, dst) in enumerate(((ov, upt), (an, aot), (mo, mut)))]
+def finish(ov, an, mo, x_v, xt, mbl, mfl, hg, upt, aot, mut, gp, ol, sem):
+    R = LAST_ROWS
+    end = FIRST_ROW + R
+    rows = pl.ds(FIRST_ROW, R)
+    moves = [(an, aot), (mo, mut)]
+    for lo, n in ((0, FIRST_ROW), (end, FFL - end)):
+        if n:
+            moves.append((ov.at[:, pl.ds(lo, n)], upt.at[:, pl.ds(lo, n)]))
+    copies = [pltpu.make_async_copy(src, dst, sem.at[k]) for k, (src, dst) in enumerate(moves)]
     for c in copies:
         c.start()
-    for c in copies:
+    for i in range(4):
+        tk = pl.ds(i * 256, 256)
+        g = jnp.dot(mbl[...], xt[:, tk], preferred_element_type=F32) * SCALE
+        gp[pl.ds(0, R), tk], gp[pl.ds(R, R), tk] = pair_grad(g, hg[rows, tk].astype(F32), R)
+    for zz in range(8):
+        cols = pl.ds(zz * 256, 256)
+        wg = jnp.dot(gp[...], x_v[:, cols], preferred_element_type=F32) * SCALE
+        for p in range(2):
+            ol[p, :, cols] = (mfl[pl.ds(p * R, R), cols] - wg[p * R:(p + 1) * R]).astype(BF16)
+    last = pltpu.make_async_copy(ol, upt.at[:, rows], sem.at[4])
+    last.start()
+    for c in copies + [last]:
         c.wait()
 
 
@@ -309,20 +340,24 @@
     most = max(r[0] for r in CHUNKS)
     dma = pltpu.SemaphoreType.DMA
     hbm = pl.BlockSpec(memory_space=pl.ANY)
-    up, an, mo = pl.pallas_call(
+    vmem = pl.BlockSpec(memory_space=pltpu.VMEM)
+    held = pl.pallas_call(
         kernel,
         name="outer_inner_step",
         out_shape=(
             pltpu.VMEM((2, FFL, D), BF16),
             pltpu.VMEM((2, FFL, 128), F32),
             pltpu.VMEM((2, FFL, 128), F32),
+            pltpu.VMEM((TOK, D), BF16),
+            pltpu.VMEM((D, TOK), BF16),
+            pltpu.VMEM((2 * LAST_ROWS, D), BF16),
+            pltpu.VMEM((2 * LAST_ROWS, D), F32),
+            pltpu.VMEM((FFL, TOK), BF16),
         ),
         in_specs=[hbm] * 5,
-        out_specs=(pl.BlockSpec(memory_space=pltpu.VMEM),) * 3,
+        out_specs=(vmem,) * 8,
         scratch_shapes=[
-            pltpu.VMEM((TOK, D), BF16),
             pltpu.VMEM((8, 2, FFL, 256), BF16),
-            pltpu.VMEM((FFL, TOK), BF16),
             pltpu.VMEM((8, 2, FFL, 256), BF16),
             pltpu.VMEM((8, 2, FFL, 256), BF16),
             pltpu.VMEM((8, 2, FFL, 128), BF16),
@@ -334,7 +369,6 @@
             pltpu.VMEM((2, FFL, 128), F32),
             pltpu.VMEM((2 * most, D), BF16),
             pltpu.VMEM((2 * most, TOK), BF16),
-            pltpu.VMEM((D, TOK), BF16),
             dma((12,)),
             dma((15,)), dma((15,)),
             dma((n, 8)), dma((n, 8)),
@@ -343,7 +377,7 @@
             dma((n, 8)), dma((n,)),
         ],
         compiler_params=pltpu.CompilerParams(
-            collective_id=0, has_side_effects=True, vmem_limit_bytes=52 << 20),
+            collective_id=0, has_side_effects=True, vmem_limit_bytes=45 << 20),
         cost_estimate=pl.CostEstimate(flops=4 * TOK * 2 * FFL * D, bytes_accessed=11_000_000, transcendentals=TOK * FFL),
     )(
         tokens[0],
@@ -353,18 +387,22 @@
         momentum.transpose(1, 2, 0),
     )
     up, an, mo = pl.pallas_call(
-        store,
-        name="store",
+        finish,
+        name="finish",
         out_shape=(
             jax.ShapeDtypeStruct((2, FFL, D), BF16),
             jax.ShapeDtypeStruct((2, FFL, 128), F32),
             jax.ShapeDtypeStruct((2, FFL, 128), F32),
         ),
-        in_specs=[pl.BlockSpec(memory_space=pltpu.VMEM)] * 3,
+        in_specs=[vmem] * 8,
         out_specs=(hbm,) * 3,
-        scratch_shapes=[dma((3,))],
-        compiler_params=pltpu.CompilerParams(vmem_limit_bytes=8 << 20),
-    )(*(pltpu.with_memory_space_constraint(a, pltpu.VMEM) for a in (up, an, mo)))
+        scratch_shapes=[
+            pltpu.VMEM((2 * LAST_ROWS, TOK), BF16),
+            pltpu.VMEM((2, LAST_ROWS, D), BF16),
+            dma((5,)),
+        ],
+        compiler_params=pltpu.CompilerParams(vmem_limit_bytes=12 << 20),
+    )(*(pltpu.with_memory_space_constraint(a, pltpu.VMEM) for a in held))
     return (up.transpose(2, 0, 1)[None], an.transpose(2, 0, 1), mo.transpose(2, 0, 1))
 
 

time: 77.7 us -> 76.3 us (0.982)
  Pallas kernels: 76.9 us -> 75.3 us
    pallas_call x1, Pallas kernels: 74.7 us -> 72.5 us  [body(): pl.pallas_call(kernel, name='outer_inner_step', out_shape=(pltpu.VMEM((2,...]
where the time goes in v4:
time: 76.3 us; the launch traced here: 76.1 us
  Pallas kernels  75.3 us (99%)
  between operations  0.8 us (1%)
    pallas_call x1, Pallas kernels, body(): pl.pallas_call(kernel, name='outer_inner_step', out_shape=(pltpu.VMEM((2,...  72.5 us
    pallas_call x1, Pallas kernels, body(): pl.pallas_call(finish, name='finish', out_shape=(jax.ShapeDtypeStruct((2,...  2.78 us

profile of v4, /device:TPU:8, one launch (start us, length us, event | category | flops | bytes accessed | tf_op | source)
XLA Modules:
  0.0 76.1 jit_solution(1581111257826012710)
XLA Ops:
  0.6 72.5 %outer_inner_step.1 = (bf16[2,448,2048]{2,1,0:T(8,128)(2,1)S(1)}, f32[2,448,128]{2,1,0:T(8,128)S(1)}, f32[2,448,128]{2,1,0:T(8,128)S(1)}, bf16[1024,2048]{1,0:T(...) custom-call(bf16[128,1024]{1,0:T(8,128)(2,1)} %bitcast.21, ...), custom_call_target="tpu_custom_call" | custom-call | flops 7516192768 | bytes 11000000 | tf_op jit(solution)/shard_map/outer_inner_step/pallas_call | solution.py:344
  73.1 2.8 %finish.1 = (bf16[2,448,2048]{2,1,0:T(8,128)(2,1)}, f32[2,448,128]{2,1,0:T(8,128)}, f32[2,448,128]{2,1,0:T(8,128)}) custom-call(bf16[2,448,2048]{2,1,0:T(8,128)(2,1)S(1)} %get-tuple-element.14.ov, f32[2,448,128]{2,1,0:T(8,128)S(1)} %get-tuple-element.15.an, f32[2,448,128]{2,1,0:T(8,128)S(1)} %get-tuple-element.16.mo, ...), custom_call_target="tpu_custom_call" | custom-call | tf_op jit(solution)/shard_map/finish/pallas_call | solution.py:389

commit v5 on v4

--- a/solution.py
+++ b/solution.py
@@ -313,10 +313,11 @@
     R = LAST_ROWS
     end = FIRST_ROW + R
     rows = pl.ds(FIRST_ROW, R)
-    moves = [(an, aot), (mo, mut)]
+    moves = []
     for lo, n in ((0, FIRST_ROW), (end, FFL - end)):
         if n:
             moves.append((ov.at[:, pl.ds(lo, n)], upt.at[:, pl.ds(lo, n)]))
+    moves += [(an, aot), (mo, mut)]
     copies = [pltpu.make_async_copy(src, dst, sem.at[k]) for k, (src, dst) in enumerate(moves)]
     for c in copies:
         c.start()
@@ -329,9 +330,12 @@
         wg = jnp.dot(gp[...], x_v[:, cols], preferred_element_type=F32) * SCALE
         for p in range(2):
             ol[p, :, cols] = (mfl[pl.ds(p * R, R), cols] - wg[p * R:(p + 1) * R]).astype(BF16)
-    last = pltpu.make_async_copy(ol, upt.at[:, rows], sem.at[4])
-    last.start()
-    for c in copies + [last]:
+        if zz % 2 == 1:
+            done = pl.ds(zz * 256 - 256, 512)
+            last = pltpu.make_async_copy(ol.at[:, :, done], upt.at[:, rows, done], sem.at[4 + zz // 2])
+            last.start()
+            copies.append(last)
+    for c in copies:
         c.wait()
 
 
@@ -399,7 +403,7 @@
         scratch_shapes=[
             pltpu.VMEM((2 * LAST_ROWS, TOK), BF16),
             pltpu.VMEM((2, LAST_ROWS, D), BF16),
-            dma((5,)),
+            dma((8,)),
         ],
         compiler_params=pltpu.CompilerParams(vmem_limit_bytes=12 << 20),
     )(*(pltpu.with_memory_space_constraint(a, pltpu.VMEM) for a in held))

time: 76.3 us -> 76.5 us (level)
  no operation moved by 1% of the time
where the time goes in v5:
time: 76.5 us; the launch traced here: 76.3 us
  Pallas kernels  75.5 us (99%)
  between operations  0.8 us (1%)
    pallas_call x1, Pallas kernels, body(): pl.pallas_call(kernel, name='outer_inner_step', out_shape=(pltpu.VMEM((2,...  72.5 us
    pallas_call x1, Pallas kernels, body(): pl.pallas_call(finish, name='finish', out_shape=(jax.ShapeDtypeStruct((2,...  3 us

profile of v5, /device:TPU:8, one launch (start us, length us, event | category | flops | bytes accessed | tf_op | source)
XLA Modules:
  0.0 76.3 jit_solution(5133253009959783618)
XLA Ops:
  0.6 72.5 %outer_inner_step.1 = (bf16[2,448,2048]{2,1,0:T(8,128)(2,1)S(1)}, f32[2,448,128]{2,1,0:T(8,128)S(1)}, f32[2,448,128]{2,1,0:T(8,128)S(1)}, bf16[1024,2048]{1,0:T(...) custom-call(bf16[128,1024]{1,0:T(8,128)(2,1)} %bitcast.21, ...), custom_call_target="tpu_custom_call" | custom-call | flops 7516192768 | bytes 11000000 | tf_op jit(solution)/shard_map/outer_inner_step/pallas_call | solution.py:348
  73.1 3.0 %finish.1 = (bf16[2,448,2048]{2,1,0:T(8,128)(2,1)}, f32[2,448,128]{2,1,0:T(8,128)}, f32[2,448,128]{2,1,0:T(8,128)}) custom-call(bf16[2,448,2048]{2,1,0:T(8,128)(2,1)S(1)} %get-tuple-element.14.ov, f32[2,448,128]{2,1,0:T(8,128)S(1)} %get-tuple-element.15.an, f32[2,448,128]{2,1,0:T(8,128)S(1)} %get-tuple-element.16.mo, ...), custom_call_target="tpu_custom_call" | custom-call | tf_op jit(solution)/shard_map/finish/pallas_call | solution.py:393
